TPU v7x, 32 devices: a whole 2x2x4 slice. The times are simulated.
32 devices in a mesh: parts: 2 (over y), expert: 4 (over x, core), split: 4 (over z).
Axes of the slice: x: 2, y: 2, z: 4, core: 2. Of those that a mesh axis runs over, the one named last changes fastest.
Arguments:
- tokens: bfloat16 [128, 7168], P(('parts', 'expert', 'split')), parts along dimension 0, may hold values from -6 to 6
- routes: int32 [128, 8], P(('parts', 'expert', 'split')), parts along dimension 0, may hold values from 0 to 15, all different within a row; in each aligned block of 4 rows (0 to 3, 4 to 7, ...) at most 4 rows name the same one
- gates: float32 [128, 8], P(('parts', 'expert', 'split')), parts along dimension 0, may hold values from 0.1 to 1
- w_gate: bfloat16 [16, 7168, 2048], P('expert', None, 'split'), may hold values from -0.0625 to 0.0625
- w_up: bfloat16 [16, 7168, 2048], P('expert', None, 'split'), may hold values from -0.0625 to 0.0625
- w_down: bfloat16 [16, 2048, 7168], P('expert', 'split'), may hold values from -0.125 to 0.125
Outputs:
- mixed: bfloat16 [128, 7168], P(('parts', 'expert', 'split')), parts along dimension 0
There are 2 independent parts, one for each index of `parts`. A program takes and returns all parts, laid end to end along the dimension named above; an argument that names none is the same for every part. Nothing has to cross between parts.
Inputs may be any that keep to these rules, and one draw needn't show every extreme that they name: `routes`: each row names 8 different experts.
All inputs are finite; a program needn't handle non-finite values.
Results may differ from a plain program's by a relative error of at most 0.0058.
Values may be sent and summed in bfloat16 or wider, within the bound.
A program may use at most 320 MiB of HBM per device.

v0:
```python
import jax
import jax.numpy as jnp
from jax import lax
from jax.sharding import PartitionSpec as P


def slot_table(chosen, experts):
    member = jnp.any(chosen[..., None] == jnp.arange(experts, dtype=jnp.int32), axis=2).astype(
        jnp.int32
    )
    before = jnp.cumsum(member, axis=1) - member
    return jnp.take_along_axis(before, chosen, axis=2)


def fill_buffer(rows_in, chosen, experts):
    blocks, count, width = rows_in.shape
    slots = slot_table(chosen, experts)
    block_ids = lax.broadcasted_iota(jnp.int32, chosen.shape, 0)
    spread = jnp.broadcast_to(rows_in[:, :, None, :], (blocks, count, chosen.shape[2], width))
    buffer = jnp.zeros((experts, blocks, count, width), jnp.bfloat16)
    return buffer.at[chosen, block_ids, slots].set(spread)


def hidden_work(received, w_gate, w_up):
    gate = jnp.einsum("njsmd,jdf->njsmf", received, w_gate, preferred_element_type=jnp.float32)
    up = jnp.einsum("njsmd,jdf->njsmf", received, w_up, preferred_element_type=jnp.float32)
    return (jax.nn.silu(gate) * up).astype(jnp.bfloat16)


def shards(tokens, routes, gates, w_gate, w_up, w_down):
    n_expert = lax.axis_size("expert")
    local = w_gate.shape[0]
    experts = n_expert * local
    count, width = tokens.shape
    buffer = fill_buffer(tokens[None], routes[None], experts)
    buffer = buffer.reshape(n_expert, local, count, width)
    arrived = lax.all_to_all(buffer, "expert", split_axis=0, concat_axis=0, tiled=True)
    received = lax.all_gather(arrived[:, :, None], "split", axis=2, tiled=True)
    hidden = hidden_work(received, w_gate, w_up)
    partial_value = jnp.einsum(
        "njsmf,jfd->njsmd", hidden, w_down, preferred_element_type=jnp.float32
    )
    summed = lax.psum_scatter(partial_value, "split", scatter_dimension=2, tiled=True).astype(
        jnp.bfloat16
    )
    results = lax.all_to_all(summed, "expert", split_axis=0, concat_axis=0, tiled=True)
    flat = results.reshape(experts * count, width)
    own_slots = slot_table(routes[None], experts)[0]
    picked = flat[routes * count + own_slots].astype(jnp.float32)
    mixed = jnp.sum(gates[:, :, None] * picked, axis=1)
    return mixed.astype(jnp.bfloat16)


def solution(mesh):
    in_specs = (
        P(("parts", "expert", "split"), None),
        P(("parts", "expert", "split"), None),
        P(("parts", "expert", "split"), None),
        P("expert", None, "split"),
        P("expert", None, "split"),
        P("expert", "split", None),
    )
    out_specs = P(("parts", "expert", "split"), None)
    return jax.shard_map(shards, mesh=mesh, in_specs=in_specs, out_specs=out_specs, check_vma=False)
```

profile of v0, /device:TPU:0, one launch (start us, length us, event | category | flops | bytes accessed | tf_op | source)
XLA Modules:
  0.0 443.8 jit_solution(2837931806647778213)
XLA Ops:
  6.5 0.0 copy-start
  6.5 0.0 all-gather.3.cloned.1.call-start
  6.5 0.8 fusion.32
  7.3 0.7 bitcast_or_fusion
  8.1 0.1 reshape.106
  8.1 0.8 gather_fusion.1
  8.9 0.0 copy-start.3
  8.9 0.1 reshape.109
  9.0 0.7 compare_select_fusion.1
  9.7 0.7 fusion.36
  10.4 0.1 pad.1.clone
  10.4 0.1 add_bitcast_fusion
  10.5 0.1 reshape.87
  10.6 0.0 copy-done
  10.7 0.2 broadcast.69
  10.9 8.0 %scatter_fusion = bf16[16,4,7168]{2,1,0:T(4,128)(2,1)S(1)} fusion(bf16[16,4,7168]{2,1,0:T(4,128)(2,1)S(1)} %broadcast.69, s32[32]{0:T(128)S(1)} %reshape.87, bf16[32,7168]{1,0:T(8,128)(2,1)S(1)} %broadcast_bitcast_fusion), kind=kCustom, calls=%fused_computation.2 | custom fusion | bytes 1376512 | tf_op jit(solution)/shard_map/scatter | solution.py:21
  18.9 17.1 %all_to_all.10 = bf16[4,4,4,7168]{3,2,1,0:T(4,128)(2,1)S(1)} all-to-all(bf16[4,4,4,7168]{3,2,1,0:T(4,128)(2,1)S(1)} %bitcast.81), channel_id=1, replica_groups=mesh['parts'=2,'expert'=4,'split'=4] {'expert'}, dimensions={0} | all-to-all | bytes 1835008 | tf_op jit(solution)/shard_map/all_to_all | solution.py:37
  36.0 1.4 copy.12
  37.4 0.0 all-gather.3.cloned.1.call-update
  37.4 0.0 copy-done.3
  37.4 0.6 dynamic-slice
  38.0 72.0 %all-gather.3.cloned.1.call-done = bf16[4,4,16,7168]{3,1,0,2:T(4,128)(2,1)} async-done(((bf16[4,4,4,7168]{3,1,0,2:T(4,128)(2,1)}), bf16[4,4,16,7168]{3,1,0,2:T(4,128)(2,1)}) %all-gather.3.cloned.1.call-update) | async-done | bytes 3670032 | tf_op jit(solution)/shard_map/all_gather | solution.py:38
  110.0 19.3 %fusion.11 = f32[4,4,4,4,512]{4,3,2,0,1:T(4,128)S(1)} fusion(bf16[4,7168,512]{2,1,0:T(8,128)(2,1)} %param.11, bf16[4,4,4,4,7168]{4,1,0,3,2:T(4,128)(2,1)} %bitcast.82), kind=kOutput, calls=%fused_computation.13 | convolution fusion | flops 1879048192 | bytes 33554432 | tf_op jit(solution)/shard_map/njsmd,jdf->njsmf/dot_general | solution.py:25
  129.3 19.6 %fusion.26 = bf16[4,4,4,4,512]{4,3,2,0,1:T(4,128)(2,1)S(1)} fusion(bf16[4,7168,512]{2,1,0:T(8,128)(2,1)} %param.12, bf16[4,4,4,4,7168]{4,1,0,3,2:T(4,128)(2,1)} %bitcast.83, f32[4,4,4,4,512]{4,3,2,0,1:T(4,128)S(1)} %fusion.11), kind=kOutput, calls=%fused_computation.16 | convolution fusion | flops 1879834624 | bytes 33816576 | tf_op jit(solution)/shard_map/njsmd,jdf->njsmf/dot_general | solution.py:26
  148.9 18.3 %fusion.6 = f32[4,4,4,4,7168]{4,3,2,0,1:T(4,128)} fusion(bf16[4,4,4,4,512]{4,3,2,0,1:T(4,128)(2,1)S(1)} %fusion.26, bf16[4,512,7168]{2,1,0:T(8,128)(2,1)} %param.13), kind=kOutput, calls=%fused_computation.9 | convolution fusion | flops 1879048192 | bytes 36962304 | tf_op jit(solution)/shard_map/njsmf,jfd->njsmd/dot_general | solution.py:40
  167.2 0.0 copy-start.1
  167.2 247.6 %all-reduce.2 = bf16[4,4,4,4,7168]{4,3,2,0,1:T(4,128)(2,1)} all-reduce(f32[4,4,4,4,7168]{4,3,2,0,1:T(4,128)} %fusion.6), channel_id=3, replica_groups=mesh['parts'=2,'expert'=4,'split'=4] {'split'}, use_global_device_ids=true, to_apply=%region_3.5.clone | all-reduce | flops 1835008 | bytes 11010048
  414.8 0.0 copy-start.2
  414.8 2.2 dynamic-slice_convert_fusion
  417.0 1.3 copy.14
  418.3 3.5 all-to-all-start.1
  421.8 0.1 reshape.77
  421.9 13.0 %all-to-all-done.1 = bf16[4,4,1,4,7168]{4,3,2,1,0:T(4,128)(2,1)S(1)} async-done(((bf16[4,4,1,4,7168]{4,3,2,1,0:T(4,128)(2,1)}), bf16[4,4,1,4,7168]{4,3,2,1,0:T(4,128)(2,1)S(1)}, u32[]{:S(2)}, u32[]{:S(2)}) %all-to-all-start.1) | async-done | bytes 917536 | tf_op jit(solution)/shard_map/all_to_all | solution.py:46
  434.9 0.2 reshape.65
  435.1 0.8 gather_fusion
  435.9 0.0 copy-done.2
  435.9 1.1 fusion.31
  437.0 0.0 copy-done.1
  (6 shorter events, 0.1 us)
Async XLA Ops:
  6.5 4.1 copy-start
  6.5 103.5 %all-gather.3.cloned.1.call-start = ((), (), s32[]{:S(2)}) async-start(), calls=%async_computation.2 | async-start | bytes 4587520 | tf_op jit(solution)/shard_map/all_gather | solution.py:38
  8.9 28.5 %copy-start.3 = (u32[32]{0:T(128)S(1)}, u32[32]{0:T(128)}, u32[]{:S(2)}) copy-start(u32[32]{0:T(128)} %constant.77) | copy-start | bytes 388
  167.2 269.8 %copy-start.1 = (bf16[4,7168]{1,0:T(4,128)(2,1)S(1)}, bf16[4,7168]{1,0:T(4,128)(2,1)}, u32[]{:S(2)}) copy-start(bf16[4,7168]{1,0:T(4,128)(2,1)} %param.8) | copy-start | bytes 172036
  414.8 21.1 %copy-start.2 = (f32[4,8]{1,0:T(4,128)S(1)}, f32[4,8]{1,0:T(4,128)}, u32[]{:S(2)}) copy-start(f32[4,8]{1,0:T(4,128)} %param.10) | copy-start | bytes 388
  418.3 16.6 %all-to-all-start.1 = ((bf16[4,4,1,4,7168]{4,3,2,1,0:T(4,128)(2,1)}), bf16[4,4,1,4,7168]{4,3,2,1,0:T(4,128)(2,1)S(1)}, u32[]{:S(2)}, u32[]{:S(2)}) async-start(bf16[4,4,1,4,7168]{4,3,2,1,0:T(4,128)(2,1)} %copy.14), calls=%async_computation.1 | async-start | bytes 1835008 | tf_op jit(solution)/shard_map/all_to_all | solution.py:46
Sparse Core Ops, SparseCore 0:
  37.6 72.4 all-gather.2
where the time goes:
time: 444 us
  blocking collectives  265 us (60%)
  waiting for transfers between devices  85 us (19%)
  matrix products  57.2 us (13%)
  local copies, waits for them, and re-layouts  15.9 us (4%)
  between operations  13.5 us (3%)
    unnamed x1, blocking collectives  248 us
    all_gather x1, waiting for transfers between devices, shards(): received = lax.all_gather(arrived[:, :, None], 'split', axis=2, tiled=True)  72 us
    dot_general x1, matrix products, hidden_work(): jnp.einsum('njsmd,jdf->njsmf', received, w_up, preferred_element_type=jnp...  19.6 us
    dot_general x1, matrix products, hidden_work(): jnp.einsum('njsmd,jdf->njsmf', received, w_gate, preferred_element_type=j...  19.3 us
    dot_general x1, matrix products, shards(): jnp.einsum('njsmf,jfd->njsmd', hidden, w_down, preferred_element_type=jnp...  18.3 us
    all_to_all x1, blocking collectives, shards(): lax.all_to_all(buffer, 'expert', split_axis=0, concat_axis=0, tiled=True)  17.1 us
    all_to_all x1, waiting for transfers between devices, shards(): lax.all_to_all(summed, 'expert', split_axis=0, concat_axis=0, tiled=True)  13 us
  transfers between devices with their start and end apart: 2, of which 2 were waited for; matrix products, arithmetic and copies ran while one was open for 0% of the time, Pallas kernels for 0%

commit v1 on v0

v1 whole, which is shorter than its diff:
```python
import functools

import jax
import jax.numpy as jnp
from jax import lax
from jax.experimental import pallas as pl
from jax.experimental.pallas import tpu as pltpu
from jax.sharding import PartitionSpec as P

MESH = pl.DeviceIdType.MESH
F32, BF16 = jnp.float32, jnp.bfloat16


def selector(rows, columns, factor, offset):
    r = lax.broadcasted_iota(jnp.int32, (rows, columns), 0)
    c = lax.broadcasted_iota(jnp.int32, (rows, columns), 1)
    hit = (c == r * factor + offset) if factor > 0 else (r == c * (-factor) + offset)
    return jnp.where(hit, F32(1), F32(0)).astype(BF16)


def kernel(
    cfg, own_ref, wg_ref, wu_ref, wd_ref, out_ref,
    buf, xs, wts, gu, dn, acc_g, acc_u, hid, part, part2,
    s1, r1, s2, r2, s3, r3,
    gu_sem, dn_sem, agz_sem, agx_sem, agc_sem, ag_recv,
    s1_sem, r1_sem, s2_sem, r2_sem, s3_sem, r3_sem,
):
    NX, NZ, NCORE, R, Q, EL, NG, ND, NC, C, FF = (
        cfg[k] for k in ("NX", "NZ", "NCORE", "R", "Q", "EL", "NG", "ND", "NC", "C", "FF")
    )
    KC = xs.shape[2]
    M = xs.shape[1]
    NGU = EL * Q
    p = lax.axis_index("parts")
    ex = lax.axis_index("expert")
    z = lax.axis_index("split")
    x, core = ex // NCORE, ex % NCORE
    other = (core + 1) % NCORE

    def dev(xx, cc, zz):
        return (p, xx * NCORE + cc, zz)

    def shard(xx, cc, zz):
        return (cc * NX + xx) * NZ + zz

    def gu_copy(i, which):
        e, q = i // Q, i % Q
        src = (wg_ref, wu_ref)[which]
        slot = i % NG
        return pltpu.make_async_copy(
            src.at[e, pl.ds(q * KC, KC), :], gu.at[slot, which], gu_sem.at[slot, which]
        )

    def dn_copy(c):
        slot = c % ND
        return pltpu.make_async_copy(
            wd_ref.at[:, :, pl.ds(pl.multiple_of(c * C, C), C)], dn.at[slot], dn_sem.at[slot]
        )

    for i in range(NG):
        gu_copy(i, 0).start()
        gu_copy(i, 1).start()

    peers = [dev(x, core, (z + k) % NZ) for k in range(1, NZ)]
    peers += [dev((x + k) % NX, core, z) for k in range(1, NX)]
    peers += [dev(x, other, z)]
    barrier = pltpu.get_barrier_semaphore()
    for peer in peers:
        pl.semaphore_signal(barrier, inc=1, device_id=peer, device_id_type=MESH)

    own = shard(x, core, z)
    buf[own] = own_ref[...]
    pl.semaphore_wait(barrier, len(peers))

    def remote(src, dst, send, recv, to):
        return pltpu.make_async_remote_copy(
            src_ref=src, dst_ref=dst, send_sem=send, recv_sem=recv, device_id=to, device_id_type=MESH
        )

    def ag(s, send, to):
        return remote(buf.at[s], buf.at[s], send, ag_recv.at[s], to)

    sends = []

    def go(copy):
        copy.start()
        sends.append(copy)

    def to_x(j):
        s = shard(x, core, (z + j) % NZ)
        for k in range(1, NX):
            go(ag(s, agx_sem.at[j, k - 1], dev((x + k) % NX, core, z)))

    def to_core(i, j):
        s = shard((x + i) % NX, core, (z + j) % NZ)
        go(ag(s, agc_sem.at[i, j], dev(x, other, z)))

    def arrived(s):
        ag(s, agz_sem.at[0], dev(x, other, z)).wait_recv()

    for k in range(1, NZ):
        go(ag(own, agz_sem.at[k - 1], dev(x, core, (z + k) % NZ)))
    to_x(0)
    to_core(0, 0)
    for j in range(1, NZ):
        arrived(shard(x, core, (z + j) % NZ))
        to_x(j)
        to_core(0, j)
    for j in range(NZ):
        for i in range(1, NX):
            arrived(shard((x + i) % NX, core, (z + j) % NZ))
            to_core(i, j)
    for i in range(NX):
        for j in range(NZ):
            arrived(shard((x + i) % NX, other, (z + j) % NZ))

    S = NX * NZ * NCORE
    G = min(S, 16)
    for g in range(S // G):
        rows = pl.ds(g * G * R, G * R)
        block = buf[g * G : (g + 1) * G].reshape(G * R * Q, buf.shape[2])
        weight = None
        for q in range(Q):
            pick = selector(G * R, G * R * Q, Q, q)
            got = jnp.dot(pick, block, preferred_element_type=F32)
            xs[q, rows, :] = got[:, :KC].astype(BF16)
            tail = got[:, KC:]
            weight = tail if weight is None else weight + tail
        wts[rows, :] = weight

    def gu_step(i, carry):
        e, q = i // Q, i % Q
        slot = i % NG
        gu_copy(i, 0).wait()
        gu_copy(i, 1).wait()
        rows = xs[q]
        g = jnp.dot(rows, gu[slot, 0], preferred_element_type=F32)
        u = jnp.dot(rows, gu[slot, 1], preferred_element_type=F32)

        @pl.when(q == 0)
        def _():
            acc_g[...] = g
            acc_u[...] = u

        @pl.when(q > 0)
        def _():
            acc_g[...] += g
            acc_u[...] += u

        @pl.when(q == Q - 1)
        def _():
            lane = lax.broadcasted_iota(jnp.int32, wts.shape, 1)
            scale = jnp.sum(jnp.where(lane == ex * EL + e, wts[...], F32(0)), axis=1, keepdims=True)
            gate = acc_g[...]
            hid[e] = (gate / (1 + jnp.exp(-gate)) * acc_u[...] * scale).astype(BF16)

        nxt = i + NG

        @pl.when(nxt < NGU)
        def _():
            gu_copy(nxt, 0).start()
            gu_copy(nxt, 1).start()

        @pl.when((nxt >= NGU) & (nxt - NGU < ND))
        def _():
            dn_copy(nxt - NGU).start()

        return carry

    lax.fori_loop(0, NGU, gu_step, 0)
    for c in range(NG, ND):
        dn_copy(c).start()

    def send1(c):
        return remote(s1.at[c], r1.at[c], s1_sem.at[c], r1_sem.at[c], dev(x, other, z))

    def send2(c, k):
        return remote(
            s2.at[c, k - 1], r2.at[c, k - 1], s2_sem.at[c, k - 1], r2_sem.at[c, k - 1],
            dev((x + k) % NX, core, z),
        )

    def send3(c, k):
        to = (z + k) % NZ
        return remote(
            s3.at[c, to], r3.at[c, k - 1], s3_sem.at[c, k - 1], r3_sem.at[c, k - 1], dev(x, core, to)
        )

    def down_step(t, carry):
        @pl.when(t < NC)
        def _():
            dn_copy(t).wait()
            slot = t % ND
            total = jnp.dot(hid[0], dn[slot, 0], preferred_element_type=F32)
            for e in range(1, EL):
                total += jnp.dot(hid[e], dn[slot, e], preferred_element_type=F32)
            part[t % 2] = total.reshape(part.shape[1:])
            s1[t] = part[t % 2, other].astype(BF16)
            send1(t).start()

            @pl.when(t + ND < NC)
            def _():
                dn_copy(t + ND).start()

        @pl.when((t >= 1) & (t <= NC))
        def _():
            c = t - 1
            send1(c).wait_recv()
            y = part[c % 2, core] + r1[c].astype(F32)
            part2[c % 2] = y.reshape(part2.shape[1:])
            for k in range(1, NX):
                s2[c, k - 1] = part2[c % 2, (x + k) % NX].astype(BF16)
                send2(c, k).start()

        @pl.when((t >= 2) & (t <= NC + 1))
        def _():
            c = t - 2
            y = part2[c % 2, x]
            for k in range(1, NX):
                send2(c, k).wait_recv()
                y += r2[c, k - 1].astype(F32)
            y = y.astype(BF16)
            w = C // Q
            packed = None
            for q in range(Q):
                pick = selector(NZ * R * Q, NZ * R, -Q, q)
                term = jnp.dot(pick, y[:, q * w : (q + 1) * w], preferred_element_type=F32)
                packed = term if packed is None else packed + term
            s3[c] = packed.astype(BF16).reshape(NZ, R * Q, w)
            for k in range(1, NZ):
                send3(c, k).start()

        @pl.when(t >= 3)
        def _():
            c = t - 3
            y = s3[c, z].astype(F32)
            for k in range(1, NZ):
                send3(c, k).wait_recv()
                y += r3[c, k - 1].astype(F32)
            out_ref[c] = y.astype(BF16)

        return carry

    lax.fori_loop(0, NC + 3, down_step, 0)

    for copy in sends:
        copy.wait_send()

    def finish(c, carry):
        send1(c).wait_send()
        for k in range(1, NX):
            send2(c, k).wait_send()
        for k in range(1, NZ):
            send3(c, k).wait_send()
        return carry

    lax.fori_loop(0, NC, finish, 0)


def shards(tokens, routes, gates, w_gate, w_up, w_down):
    n_expert, n_split = lax.axis_size("expert"), lax.axis_size("split")
    R, D = tokens.shape
    EL, _, FF = w_gate.shape
    experts = n_expert * EL
    Q = 16 // R
    NCORE = 2
    NX, NZ = n_expert // NCORE, n_split
    KC = D // Q
    C = 1024
    NC = D // C
    NG, ND = min(7, EL * Q), min(5, NC)
    M = NX * NZ * NCORE * R
    S = NX * NZ * NCORE
    cfg = dict(NX=NX, NZ=NZ, NCORE=NCORE, R=R, Q=Q, EL=EL, NG=NG, ND=ND, NC=NC, C=C, FF=FF)

    named = routes[:, :, None] == jnp.arange(experts, dtype=jnp.int32)
    weight = jnp.sum(jnp.where(named, gates[:, :, None], F32(0)), axis=1)
    hi = lax.reduce_precision(weight, 8, 7)
    mid = lax.reduce_precision(weight - hi, 8, 7)
    low = weight - hi - mid
    terms = jnp.stack([hi, mid, low] + [jnp.zeros_like(hi)] * (Q - 3), axis=1).astype(BF16)
    terms = jnp.pad(terms, ((0, 0), (0, 0), (0, 128 - experts)))
    own = jnp.concatenate([tokens.reshape(R, Q, KC), terms], axis=2).reshape(R * Q, KC + 128)

    any_space = pl.BlockSpec(memory_space=pl.ANY)
    vmem = pl.BlockSpec(memory_space=pltpu.VMEM)
    dma = pltpu.SemaphoreType.DMA
    out = pl.pallas_call(
        functools.partial(kernel, cfg),
        out_shape=jax.ShapeDtypeStruct((NC, R * Q, C // Q), BF16),
        in_specs=[vmem, any_space, any_space, any_space],
        out_specs=vmem,
        scratch_shapes=[
            pltpu.VMEM((S, R * Q, KC + 128), BF16),
            pltpu.VMEM((Q, M, KC), BF16),
            pltpu.VMEM((M, 128), F32),
            pltpu.VMEM((NG, 2, KC, FF), BF16),
            pltpu.VMEM((ND, EL, FF, C), BF16),
            pltpu.VMEM((M, FF), F32),
            pltpu.VMEM((M, FF), F32),
            pltpu.VMEM((EL, M, FF), BF16),
            pltpu.VMEM((2, NCORE, M // NCORE, C), F32),
            pltpu.VMEM((2, NX, NZ * R, C), F32),
            pltpu.VMEM((NC, M // NCORE, C), BF16),
            pltpu.VMEM((NC, M // NCORE, C), BF16),
            pltpu.VMEM((NC, NX - 1, NZ * R, C), BF16),
            pltpu.VMEM((NC, NX - 1, NZ * R, C), BF16),
            pltpu.VMEM((NC, NZ, R * Q, C // Q), BF16),
            pltpu.VMEM((NC, NZ - 1, R * Q, C // Q), BF16),
            dma((NG, 2)), dma((ND,)), dma((NZ - 1,)), dma((NZ, NX - 1)), dma((NX, NZ)), dma((S,)),
            dma((NC,)), dma((NC,)), dma((NC, NX - 1)), dma((NC, NX - 1)), dma((NC, NZ - 1)), dma((NC, NZ - 1)),
        ],
        compiler_params=pltpu.CompilerParams(
            collective_id=0, has_side_effects=True, vmem_limit_bytes=60 * 1024 * 1024
        ),
        cost_estimate=pl.CostEstimate(
            flops=6 * M * EL * D * FF, bytes_accessed=6 * EL * D * FF, transcendentals=M * EL * FF
        ),
        name="expert_layer",
    )(own, w_gate, w_up, w_down)
    return out.reshape(NC, R, Q, C // Q).transpose(1, 0, 2, 3).reshape(R, D)


def solution(mesh):
    in_specs = (
        P(("parts", "expert", "split"), None),
        P(("parts", "expert", "split"), None),
        P(("parts", "expert", "split"), None),
        P("expert", None, "split"),
        P("expert", None, "split"),
        P("expert", "split", None),
    )
    out_specs = P(("parts", "expert", "split"), None)
    return jax.shard_map(shards, mesh=mesh, in_specs=in_specs, out_specs=out_specs, check_vma=False)
```

time: 444 us -> 60.7 us (0.14)
  blocking collectives: 265 us -> 0 us
  waiting for transfers between devices: 85 us -> 0 us
  matrix products: 57.2 us -> 0 us
  Pallas kernels: 0 us -> 56.4 us
  between operations: 13.5 us -> 0.02 us
  local copies, waits for them, and re-layouts: 15.9 us -> 2.47 us
    unnamed x1 -> x0, blocking collectives: 248 us -> none
    all_gather x1 -> x0, waiting for transfers between devices: 72 us -> none  [shards(): received = lax.all_gather(arrived[:, :, None], 'split', axis=2, tiled=True)]
    dot_general x3 -> x0, matrix products: 57.2 us -> none  [the longest x1 19.6 us: hidden_work(): jnp.einsum('njsmd,jdf->njsmf', received, w_up, preferred_element_type=jnp...]
    pallas_call x0 -> x1, Pallas kernels: none -> 56.4 us  [shards(): pl.pallas_call(functools.partial(kernel, cfg), out_shape=jax.ShapeDtypeSt...]
    all_to_all x1 -> x0, blocking collectives: 17.1 us -> none  [shards(): lax.all_to_all(buffer, 'expert', split_axis=0, concat_axis=0, tiled=True)]
    all_to_all x1 -> x0, waiting for transfers between devices: 13 us -> none  [shards(): lax.all_to_all(summed, 'expert', split_axis=0, concat_axis=0, tiled=True)]
    scatter x1 -> x0, local copies, waits for them, and re-layouts: 8.03 us -> none  [fill_buffer(): return buffer.at[chosen, block_ids, slots].set(spread)]
  transfers between devices with their start and end apart: 2 -> 0, of which waited for: 2 -> 0; matrix products, arithmetic and copies ran while one was open for 0% -> 0% of each run, Pallas kernels for 0% -> 0%
where the time goes in v1:
time: 60.7 us; the launch traced here: 60.4 us
  Pallas kernels  56.4 us (93%)
  local copies, waits for them, and re-layouts  2.47 us (4%)
  other arithmetic  1.5 us (2%)
    pallas_call x1, Pallas kernels, shards(): pl.pallas_call(functools.partial(kernel, cfg), out_shape=jax.ShapeDtypeSt...  56.4 us
    reshape x2, local copies, waits for them, and re-layouts, shards(): return out.reshape(NC, R, Q, C // Q).transpose(1, 0, 2, 3).reshape(R, D)  1.49 us

profile of v1, /device:TPU:0, one launch (start us, length us, event | category | flops | bytes accessed | tf_op | source)
XLA Modules:
  0.0 60.4 jit_solution(6869134643918237799)
XLA Ops:
  0.0 0.1 pad.10.clone
  0.1 0.8 %select_reduce_fusion = f32[4,16]{1,0:T(4,128)S(1)} fusion(f32[4,8]{1,0:T(4,128)} %param.8, s32[4,8]{1,0:T(4,128)} %param.7), kind=kLoop, calls=%fused_computation.1 | loop fusion | flops 1472 | bytes 512 | tf_op jit(solution)/shard_map/reduce_sum | solution.py:277
  0.9 0.1 maximum_maximum_fusion
  1.0 0.9 %concatenate.8 = bf16[16,1792]{1,0:T(8,128)(2,1)S(1)} reshape(bf16[4,7168]{1,0:T(4,128)(2,1)} %param.6) | data formatting | bytes 114688 | tf_op jit(solution)/shard_map/concatenate | solution.py:283
  1.8 0.6 %pad_maximum_fusion.own_ref = bf16[16,1920]{1,0:T(8,128)(2,1)} fusion(bf16[16,128]{1,0:T(8,128)(2,1)S(1)} %bitcast.11, bf16[16,1792]{1,0:T(8,128)(2,1)S(1)} %concatenate.8), kind=kLoop, calls=%fused_computation | loop fusion | flops 122880 | bytes 122880 | tf_op jit(solution)/shard_map/concatenate | solution.py:283
  2.5 56.4 %expert_layer.1 = bf16[7,16,256]{2,1,0:T(8,128)(2,1)} custom-call(bf16[16,1920]{1,0:T(8,128)(2,1)} %pad_maximum_fusion.own_ref, bf16[4,7168,512]{2,1,0:T(8,128)(2,1)} %wg_ref.1, bf16[4,7168,512]{2,1,0:T(8,128)(2,1)} %wu_ref.1, bf16[4,512,7168]{2,1,0:T(8,128)(2,1)} %wd_ref.1), custom_call_target="tpu_custom_call" | custom-call | flops 5637144576 | bytes 88080384 | tf_op jit(solution)/shard_map/expert_layer/pallas_call | solution.py:288
  58.9 0.8 %reshape.37 = bf16[7,4,4,256]{3,2,1,0:T(4,128)(2,1)S(1)} reshape(bf16[7,16,256]{2,1,0:T(8,128)(2,1)} %expert_layer.1) | data formatting | bytes 114688 | tf_op jit(solution)/shard_map/reshape | solution.py:321
  59.8 0.6 %reshape.38 = bf16[4,7168]{1,0:T(4,128)(2,1)} reshape(bf16[4,7,4,256]{3,2,1,0:T(4,128)(2,1)S(1)} %copy.10) | data formatting | bytes 114688 | tf_op jit(solution)/shard_map/reshape | solution.py:321
  (4 shorter events, 0.1 us)

commit v2 on v1

--- a/solution.py
+++ b/solution.py
@@ -9,6 +9,7 @@
 
 MESH = pl.DeviceIdType.MESH
 F32, BF16 = jnp.float32, jnp.bfloat16
+LAG = 2
 
 
 def selector(rows, columns, factor, offset):
@@ -19,7 +20,7 @@
 
 
 def kernel(
-    cfg, own_ref, wg_ref, wu_ref, wd_ref, out_ref,
+    cfg, tok_ref, routes_ref, gates_ref, wg_ref, wu_ref, wd_ref, out_ref,
     buf, xs, wts, gu, dn, acc_g, acc_u, hid, part, part2,
     s1, r1, s2, r2, s3, r3,
     gu_sem, dn_sem, agz_sem, agx_sem, agc_sem, ag_recv,
@@ -69,7 +70,23 @@
         pl.semaphore_signal(barrier, inc=1, device_id=peer, device_id_type=MESH)
 
     own = shard(x, core, z)
-    buf[own] = own_ref[...]
+    routes, gates = routes_ref[...], gates_ref[...]
+    lane = lax.broadcasted_iota(jnp.int32, (R, 128), 1)
+    rest = jnp.zeros((R, 128), F32)
+    for k in range(routes.shape[1]):
+        rest += jnp.where(routes[:, k : k + 1] == lane, gates[:, k : k + 1], F32(0))
+    mine, tail = None, None
+    for q in range(Q):
+        place = selector(R * Q, R, -Q, q)
+        term = jnp.dot(place, tok_ref[:, q * KC : (q + 1) * KC], preferred_element_type=F32)
+        mine = term if mine is None else mine + term
+        if q < 3:
+            piece = rest.astype(BF16)
+            rest = rest - piece.astype(F32)
+            term = jnp.dot(place, piece, preferred_element_type=F32)
+            tail = term if tail is None else tail + term
+    buf[own, :, :KC] = mine.astype(BF16)
+    buf[own, :, KC:] = tail.astype(BF16)
     pl.semaphore_wait(barrier, len(peers))
 
     def remote(src, dst, send, recv, to):
@@ -194,28 +211,28 @@
             total = jnp.dot(hid[0], dn[slot, 0], preferred_element_type=F32)
             for e in range(1, EL):
                 total += jnp.dot(hid[e], dn[slot, e], preferred_element_type=F32)
-            part[t % 2] = total.reshape(part.shape[1:])
-            s1[t] = part[t % 2, other].astype(BF16)
+            part[t % (LAG + 1)] = total.reshape(part.shape[1:])
+            s1[t] = part[t % (LAG + 1), other].astype(BF16)
             send1(t).start()
 
             @pl.when(t + ND < NC)
             def _():
                 dn_copy(t + ND).start()
 
-        @pl.when((t >= 1) & (t <= NC))
-        def _():
-            c = t - 1
+        @pl.when((t >= LAG) & (t < NC + LAG))
+        def _():
+            c = t - LAG
             send1(c).wait_recv()
-            y = part[c % 2, core] + r1[c].astype(F32)
-            part2[c % 2] = y.reshape(part2.shape[1:])
+            y = part[c % (LAG + 1), core] + r1[c].astype(F32)
+            part2[c % (LAG + 1)] = y.reshape(part2.shape[1:])
             for k in range(1, NX):
-                s2[c, k - 1] = part2[c % 2, (x + k) % NX].astype(BF16)
+                s2[c, k - 1] = part2[c % (LAG + 1), (x + k) % NX].astype(BF16)
                 send2(c, k).start()
 
-        @pl.when((t >= 2) & (t <= NC + 1))
-        def _():
-            c = t - 2
-            y = part2[c % 2, x]
+        @pl.when((t >= 2 * LAG) & (t < NC + 2 * LAG))
+        def _():
+            c = t - 2 * LAG
+            y = part2[c % (LAG + 1), x]
             for k in range(1, NX):
                 send2(c, k).wait_recv()
                 y += r2[c, k - 1].astype(F32)
@@ -230,18 +247,23 @@
             for k in range(1, NZ):
                 send3(c, k).start()
 
-        @pl.when(t >= 3)
-        def _():
-            c = t - 3
+        @pl.when(t >= 3 * LAG)
+        def _():
+            c = t - 3 * LAG
             y = s3[c, z].astype(F32)
             for k in range(1, NZ):
                 send3(c, k).wait_recv()
                 y += r3[c, k - 1].astype(F32)
-            out_ref[c] = y.astype(BF16)
+            y = y.astype(BF16)
+            w = C // Q
+            for q in range(Q):
+                pick = selector(R, R * Q, Q, q)
+                piece = jnp.dot(pick, y, preferred_element_type=F32).astype(BF16)
+                out_ref[:, pl.ds(pl.multiple_of(c * C + q * w, 128), w)] = piece
 
         return carry
 
-    lax.fori_loop(0, NC + 3, down_step, 0)
+    lax.fori_loop(0, NC + 3 * LAG, down_step, 0)
 
     for copy in sends:
         copy.wait_send()
@@ -261,7 +283,6 @@
     n_expert, n_split = lax.axis_size("expert"), lax.axis_size("split")
     R, D = tokens.shape
     EL, _, FF = w_gate.shape
-    experts = n_expert * EL
     Q = 16 // R
     NCORE = 2
     NX, NZ = n_expert // NCORE, n_split
@@ -273,22 +294,13 @@
     S = NX * NZ * NCORE
     cfg = dict(NX=NX, NZ=NZ, NCORE=NCORE, R=R, Q=Q, EL=EL, NG=NG, ND=ND, NC=NC, C=C, FF=FF)
 
-    named = routes[:, :, None] == jnp.arange(experts, dtype=jnp.int32)
-    weight = jnp.sum(jnp.where(named, gates[:, :, None], F32(0)), axis=1)
-    hi = lax.reduce_precision(weight, 8, 7)
-    mid = lax.reduce_precision(weight - hi, 8, 7)
-    low = weight - hi - mid
-    terms = jnp.stack([hi, mid, low] + [jnp.zeros_like(hi)] * (Q - 3), axis=1).astype(BF16)
-    terms = jnp.pad(terms, ((0, 0), (0, 0), (0, 128 - experts)))
-    own = jnp.concatenate([tokens.reshape(R, Q, KC), terms], axis=2).reshape(R * Q, KC + 128)
-
     any_space = pl.BlockSpec(memory_space=pl.ANY)
     vmem = pl.BlockSpec(memory_space=pltpu.VMEM)
     dma = pltpu.SemaphoreType.DMA
     out = pl.pallas_call(
         functools.partial(kernel, cfg),
-        out_shape=jax.ShapeDtypeStruct((NC, R * Q, C // Q), BF16),
-        in_specs=[vmem, any_space, any_space, any_space],
+        out_shape=jax.ShapeDtypeStruct((R, D), BF16),
+        in_specs=[vmem, vmem, vmem, any_space, any_space, any_space],
         out_specs=vmem,
         scratch_shapes=[
             pltpu.VMEM((S, R * Q, KC + 128), BF16),
@@ -299,8 +311,8 @@
             pltpu.VMEM((M, FF), F32),
             pltpu.VMEM((M, FF), F32),
             pltpu.VMEM((EL, M, FF), BF16),
-            pltpu.VMEM((2, NCORE, M // NCORE, C), F32),
-            pltpu.VMEM((2, NX, NZ * R, C), F32),
+            pltpu.VMEM((LAG + 1, NCORE, M // NCORE, C), F32),
+            pltpu.VMEM((LAG + 1, NX, NZ * R, C), F32),
             pltpu.VMEM((NC, M // NCORE, C), BF16),
             pltpu.VMEM((NC, M // NCORE, C), BF16),
             pltpu.VMEM((NC, NX - 1, NZ * R, C), BF16),
@@ -317,8 +329,8 @@
             flops=6 * M * EL * D * FF, bytes_accessed=6 * EL * D * FF, transcendentals=M * EL * FF
         ),
         name="expert_layer",
-    )(own, w_gate, w_up, w_down)
-    return out.reshape(NC, R, Q, C // Q).transpose(1, 0, 2, 3).reshape(R, D)
+    )(tokens, routes, gates, w_gate, w_up, w_down)
+    return out
 
 
 def solution(mesh):

time: 60.7 us -> 52.2 us (0.86)
  Pallas kernels: 56.4 us -> 50.5 us
  other arithmetic: 1.5 us -> 0 us
  local copies, waits for them, and re-layouts: 2.47 us -> 1.46 us
    pallas_call x1, Pallas kernels: 56.4 us -> 50.5 us  [shards(): pl.pallas_call(functools.partial(kernel, cfg), out_shape=jax.ShapeDtypeSt...]
    reshape x2 -> x0, local copies, waits for them, and re-layouts: 1.49 us -> none  [shards(): return out.reshape(NC, R, Q, C // Q).transpose(1, 0, 2, 3).reshape(R, D)]
    unnamed x1, local copies, waits for them, and re-layouts: 0.01 us -> 1.46 us
    concatenate x1 -> x0, local copies, waits for them, and re-layouts: 0.86 us -> none  [shards(): jnp.concatenate([tokens.reshape(R, Q, KC), terms], axis=2)]
    reduce_sum x1 -> x0, other arithmetic: 0.78 us -> none  [shards(): weight = jnp.sum(jnp.where(named, gates[:, :, None], F32(0)), axis=1)]
    concatenate x1 -> x0, other arithmetic: 0.62 us -> none  [shards(): jnp.concatenate([tokens.reshape(R, Q, KC), terms], axis=2)]
where the time goes in v2:
time: 52.2 us; the launch traced here: 52 us
  Pallas kernels  50.5 us (97%)
  local copies, waits for them, and re-layouts  1.46 us (3%)
    pallas_call x1, Pallas kernels, shards(): pl.pallas_call(functools.partial(kernel, cfg), out_shape=jax.ShapeDtypeSt...  50.5 us
    unnamed x1, local copies, waits for them, and re-layouts  1.46 us

profile of v2, /device:TPU:0, one launch (start us, length us, event | category | flops | bytes accessed | tf_op | source)
XLA Modules:
  0.0 52.0 jit_solution(16862514552320756304)
XLA Ops:
  0.0 50.5 %expert_layer.1 = bf16[4,7168]{1,0:T(4,128)(2,1)} custom-call(bf16[4,7168]{1,0:T(4,128)(2,1)} %tok_ref.1, s32[4,8]{1,0:T(4,128)} %routes_ref.1, f32[4,8]{1,0:T(4,128)} %gates_ref.1, bf16[4,7168,512]{2,1,0:T(8,128)(2,1)} %wg_ref.1, bf16[4,7168,512]{2,1,0:T(8,128)(2,1)} %wu_ref.1, bf16[4,512,7168]{2,1,0:T(8,128)(2,1)} %wd_ref.1), custom_call_target="tpu_custom_call" | custom-call | flops 5637144576 | bytes 88080384 | tf_op jit(solution)/shard_map/expert_layer/pallas_call | solution.py:300
  50.5 1.5 %copy.8 = bf16[4,7168]{1,0:T(4,128)(2,1)} copy(bf16[4,7168]{1,0:T(4,128)(2,1)} %expert_layer.1) | data formatting | bytes 114688

commit v3 on v2

--- a/solution.py
+++ b/solution.py
@@ -61,6 +61,8 @@
     for i in range(NG):
         gu_copy(i, 0).start()
         gu_copy(i, 1).start()
+    for c in range(ND):
+        dn_copy(c).start()
 
     peers = [dev(x, core, (z + k) % NZ) for k in range(1, NZ)]
     peers += [dev((x + k) % NX, core, z) for k in range(1, NX)]
@@ -103,29 +105,34 @@
         copy.start()
         sends.append(copy)
 
+    def peer_z(j):
+        if NZ != 4:
+            return (z + j) % NZ
+        return (z, z + 1 - 2 * (z % 2), (z + 2) % 4, 3 - z)[j]
+
     def to_x(j):
-        s = shard(x, core, (z + j) % NZ)
+        s = shard(x, core, peer_z(j))
         for k in range(1, NX):
             go(ag(s, agx_sem.at[j, k - 1], dev((x + k) % NX, core, z)))
 
     def to_core(i, j):
-        s = shard((x + i) % NX, core, (z + j) % NZ)
+        s = shard((x + i) % NX, core, peer_z(j))
         go(ag(s, agc_sem.at[i, j], dev(x, other, z)))
 
     def arrived(s):
         ag(s, agz_sem.at[0], dev(x, other, z)).wait_recv()
 
     for k in range(1, NZ):
-        go(ag(own, agz_sem.at[k - 1], dev(x, core, (z + k) % NZ)))
+        go(ag(own, agz_sem.at[k - 1], dev(x, core, peer_z(k))))
     to_x(0)
     to_core(0, 0)
     for j in range(1, NZ):
-        arrived(shard(x, core, (z + j) % NZ))
+        arrived(shard(x, core, peer_z(j)))
         to_x(j)
         to_core(0, j)
     for j in range(NZ):
         for i in range(1, NX):
-            arrived(shard((x + i) % NX, core, (z + j) % NZ))
+            arrived(shard((x + i) % NX, core, peer_z(j)))
             to_core(i, j)
     for i in range(NX):
         for j in range(NZ):
@@ -178,15 +185,9 @@
             gu_copy(nxt, 0).start()
             gu_copy(nxt, 1).start()
 
-        @pl.when((nxt >= NGU) & (nxt - NGU < ND))
-        def _():
-            dn_copy(nxt - NGU).start()
-
         return carry
 
     lax.fori_loop(0, NGU, gu_step, 0)
-    for c in range(NG, ND):
-        dn_copy(c).start()
 
     def send1(c):
         return remote(s1.at[c], r1.at[c], s1_sem.at[c], r1_sem.at[c], dev(x, other, z))

time: 52.2 us -> 51 us (0.977)
  Pallas kernels: 50.5 us -> 49.3 us
    pallas_call x1, Pallas kernels: 50.5 us -> 49.3 us  [shards(): pl.pallas_call(functools.partial(kernel, cfg), out_shape=jax.ShapeDtypeSt...]
where the time goes in v3:
time: 51 us; the launch traced here: 50.8 us
  Pallas kernels  49.3 us (97%)
  local copies, waits for them, and re-layouts  1.46 us (3%)
    pallas_call x1, Pallas kernels, shards(): pl.pallas_call(functools.partial(kernel, cfg), out_shape=jax.ShapeDtypeSt...  49.3 us
    unnamed x1, local copies, waits for them, and re-layouts  1.46 us

profile of v3, /device:TPU:0, one launch (start us, length us, event | category | flops | bytes accessed | tf_op | source)
XLA Modules:
  0.0 50.8 jit_solution(14173811794375698044)
XLA Ops:
  0.0 49.3 %expert_layer.1 = bf16[4,7168]{1,0:T(4,128)(2,1)} custom-call(bf16[4,7168]{1,0:T(4,128)(2,1)} %tok_ref.1, s32[4,8]{1,0:T(4,128)} %routes_ref.1, f32[4,8]{1,0:T(4,128)} %gates_ref.1, bf16[4,7168,512]{2,1,0:T(8,128)(2,1)} %wg_ref.1, bf16[4,7168,512]{2,1,0:T(8,128)(2,1)} %wu_ref.1, bf16[4,512,7168]{2,1,0:T(8,128)(2,1)} %wd_ref.1), custom_call_target="tpu_custom_call" | custom-call | flops 5637144576 | bytes 88080384 | tf_op jit(solution)/shard_map/expert_layer/pallas_call | solution.py:301
  49.3 1.5 %copy.8 = bf16[4,7168]{1,0:T(4,128)(2,1)} copy(bf16[4,7168]{1,0:T(4,128)(2,1)} %expert_layer.1) | data formatting | bytes 114688

commit v4 on v3

--- a/solution.py
+++ b/solution.py
@@ -9,7 +9,7 @@
 
 MESH = pl.DeviceIdType.MESH
 F32, BF16 = jnp.float32, jnp.bfloat16
-LAG = 2
+LAG = 4
 
 
 def selector(rows, columns, factor, offset):
@@ -288,9 +288,9 @@
     NCORE = 2
     NX, NZ = n_expert // NCORE, n_split
     KC = D // Q
-    C = 1024
+    C = 512
     NC = D // C
-    NG, ND = min(7, EL * Q), min(5, NC)
+    NG, ND = min(7, EL * Q), min(10, NC)
     M = NX * NZ * NCORE * R
     S = NX * NZ * NCORE
     cfg = dict(NX=NX, NZ=NZ, NCORE=NCORE, R=R, Q=Q, EL=EL, NG=NG, ND=ND, NC=NC, C=C, FF=FF)

time: 51 us -> 52.4 us (1.027)
  Pallas kernels: 49.3 us -> 50.7 us
    pallas_call x1, Pallas kernels: 49.3 us -> 50.7 us  [shards(): pl.pallas_call(functools.partial(kernel, cfg), out_shape=jax.ShapeDtypeSt...]
where the time goes in v4:
time: 52.4 us; the launch traced here: 52.2 us
  Pallas kernels  50.7 us (97%)
  local copies, waits for them, and re-layouts  1.46 us (3%)
    pallas_call x1, Pallas kernels, shards(): pl.pallas_call(functools.partial(kernel, cfg), out_shape=jax.ShapeDtypeSt...  50.7 us
    unnamed x1, local copies, waits for them, and re-layouts  1.46 us

profile of v4, /device:TPU:0, one launch (start us, length us, event | category | flops | bytes accessed | tf_op | source)
XLA Modules:
  0.0 52.2 jit_solution(1752276884008393857)
XLA Ops:
  0.0 50.7 %expert_layer.1 = bf16[4,7168]{1,0:T(4,128)(2,1)} custom-call(bf16[4,7168]{1,0:T(4,128)(2,1)} %tok_ref.1, s32[4,8]{1,0:T(4,128)} %routes_ref.1, f32[4,8]{1,0:T(4,128)} %gates_ref.1, bf16[4,7168,512]{2,1,0:T(8,128)(2,1)} %wg_ref.1, bf16[4,7168,512]{2,1,0:T(8,128)(2,1)} %wu_ref.1, bf16[4,512,7168]{2,1,0:T(8,128)(2,1)} %wd_ref.1), custom_call_target="tpu_custom_call" | custom-call | flops 5637144576 | bytes 88080384 | tf_op jit(solution)/shard_map/expert_layer/pallas_call | solution.py:301
  50.8 1.5 %copy.8 = bf16[4,7168]{1,0:T(4,128)(2,1)} copy(bf16[4,7168]{1,0:T(4,128)(2,1)} %expert_layer.1) | data formatting | bytes 114688
